TPU v7x, 256 devices: a whole 4x4x8 slice. The times are simulated.
256 devices in a mesh: grp: 2 (over x_hi), dp: 8 (over y, core), mp: 16 (over x_lo, z).
Axes of the slice: x: 4 (x_hi: 2, x_lo: 2; x = x_hi * 2 + x_lo), y: 4, z: 8, core: 2. Of those that a mesh axis runs over, the one named last changes fastest.
Arguments:
- hidden_in: bfloat16 [1024, 8192], P('dp'), may hold values from -6 to 6
- full_weights: bfloat16 [8192, 2, 16384], P('mp', 'grp', 'dp'), may hold values from -1 to 1, as said below
- codes: int32 [8192, 2, 16384], P('mp', None, 'dp'), may hold values from 0 to 3, as said below
- scales: float32 [64, 2, 16384], P('mp', None, 'dp'), may hold values from 0 to 1, as said below
Outputs:
- scale_grad: float32 [64, 2, 16384], P('mp', 'grp', 'dp')
Inputs may be any that keep to these rules, and one draw needn't show every extreme that they name: codes are 2-bit values. full_weights lie near the grid that codes and positive group scales span. scales are positive.
All inputs are finite; a program needn't handle non-finite values.
Results may differ from a plain program's by a relative error of at most 0.0088.
Values may be sent and summed in bfloat16 or wider, within the bound.
A program may use at most 128 MiB of HBM per device.

v0:
```python
import jax
import jax.numpy as jnp
from jax import lax
from jax.sharding import PartitionSpec as P


def swapped(x, axis, apart):
    return lax.ppermute(x, axis, [(i, i ^ 1 << apart) for i in range(lax.axis_size(axis))])


def dequantize(code_part, scale_part):
    group = code_part.shape[0] // scale_part.shape[0]
    values = jnp.repeat(scale_part, group, axis=0) * (code_part.astype(jnp.float32) - 1.5)
    return values.astype(jnp.bfloat16)


def per_device(hidden_in, full_weights, codes, scales):
    side = lax.axis_index("grp")
    is_teacher = side == 0
    width = codes.shape[0]
    units = codes.shape[2]
    column = lax.axis_index("mp")
    x_slice = lax.dynamic_slice_in_dim(hidden_in, column * width, width, 1)
    x_cols = lax.all_gather(x_slice, "dp", axis=0, tiled=True)
    total_rows = x_cols.shape[0]
    both = lax.all_gather(full_weights, "grp", axis=1, tiled=True)
    weights = jnp.where(is_teacher, both, dequantize(codes, scales))
    flat = weights.reshape(width, 2 * units)
    own_rows = total_rows // lax.axis_size("mp")
    rows = x_cols
    sums = lax.psum_scatter(
        jnp.dot(rows, flat, preferred_element_type=jnp.float32).reshape(
            lax.axis_size("mp") * own_rows, 2, units
        ),
        "mp",
        scatter_dimension=0,
        tiled=True,
    )
    partner = swapped(sums, "grp", 0)
    teacher = jnp.where(is_teacher, sums, partner)
    student = jnp.where(is_teacher, partner, sums)
    teacher_hidden = jax.nn.silu(teacher[:, 0]) * teacher[:, 1]
    gate = student[:, 0]
    upper = student[:, 1]
    difference = (jax.nn.silu(gate) * upper - teacher_hidden) / total_rows
    sig = jax.nn.sigmoid(gate)
    grad_gate = difference * upper * sig * (1.0 + gate * (1.0 - sig))
    grad_up = difference * gate * sig
    own_grads = jnp.where(is_teacher, grad_gate, grad_up).astype(jnp.bfloat16)
    rows = x_cols
    weight_grads = lax.dot_general(
        rows,
        lax.all_gather(own_grads, "mp", axis=0, tiled=True),
        (((0,), (0,)), ((), ())),
        preferred_element_type=jnp.float32,
    )
    own_offsets = lax.dynamic_index_in_dim(codes, side, 1, keepdims=False).astype(jnp.float32) - 1.5
    groups = scales.shape[0]
    summed = (weight_grads * own_offsets).reshape(groups, width // groups, units).sum(axis=1)
    return summed[:, None, :]


def solution(mesh):
    return jax.shard_map(
        per_device,
        mesh=mesh,
        in_specs=(P("dp", None), P("mp", "grp", "dp"), P("mp", None, "dp"), P("mp", None, "dp")),
        out_specs=P("mp", "grp", "dp"),
        check_vma=False,
    )
```

profile of v0, /device:TPU:8, one launch (start us, length us, event | category | flops | bytes accessed | tf_op | source)
XLA Modules:
  0.0 423.2 jit_solution(16997377908010261582)
XLA Ops:
  6.5 0.7 all-gather.6.cloned.1.call-update
  7.3 0.0 all-gather.4.cloned.1.call-start
  7.3 0.8 copy-done
  8.1 0.7 constant_dynamic-slice_fusion.1
  8.8 0.0 reduce-scatter.2.cloned.1.call-start
  8.9 1.5 copy.11
  10.4 6.1 %broadcast_in_dim.6 = f32[4,128,2,2048]{1,0,3,2:T(4,128)} broadcast(f32[4,2,2048]{0,2,1:T(8,128)S(1)} %copy.11), dimensions={0,2,3} | broadcast | bytes 8454144 | tf_op jit(solution)/shard_map/broadcast_in_dim | solution.py:13
  16.5 10.4 %reshape.14 = f32[512,2,2048]{0,2,1:T(8,128)} reshape(f32[4,128,2,2048]{1,0,3,2:T(4,128)} %broadcast_in_dim.6) | data formatting | bytes 16777216 | tf_op jit(solution)/shard_map/reshape | solution.py:13
  26.9 13.3 %copy.12 = s32[512,2,2048]{0,2,1:T(8,128)} copy(s32[512,2,2048]{2,1,0:T(2,128)} %param.6) | data formatting | bytes 16777216 | tf_op args[2]
  40.2 35.2 %all-gather.6.cloned.1.call-done = bf16[512,2,2048]{2,0,1:T(8,128)(2,1)} async-done(((bf16[512,1,2048]{2,0,1:T(8,128)(2,1)}), bf16[512,2,2048]{2,0,1:T(8,128)(2,1)}) %all-gather.6.cloned.1.call-update) | async-done | bytes 4194320 | tf_op jit(solution)/shard_map/all_gather | solution.py:26
  75.4 6.2 %copy.13 = bf16[512,2,2048]{0,2,1:T(8,128)(2,1)} copy(bf16[512,2,2048]{2,0,1:T(8,128)(2,1)} %all-gather.6.cloned.1.call-done) | data formatting | bytes 8388608 | tf_op jit(solution)/shard_map/all_gather | solution.py:26
  81.6 19.4 %all-gather.4.cloned.1.call-done = bf16[1024,512]{1,0:T(8,128)(2,1)} async-done(((bf16[128,512]{1,0:T(8,128)(2,1)}), bf16[1024,512]{1,0:T(8,128)(2,1)}) %all-gather.4.cloned.1.call-update) | async-done | bytes 1048592 | tf_op jit(solution)/shard_map/all_gather | solution.py:24
  101.0 17.7 %fusion.2 = f32[1024,2,2048]{2,0,1:T(8,128)} fusion(bf16[512,2,2048]{0,2,1:T(8,128)(2,1)} %copy.13, f32[512,2,2048]{0,2,1:T(8,128)} %reshape.14, s32[512,2,2048]{0,2,1:T(8,128)} %copy.12, pred[]{:T(512)S(6)} %eq.3, bf16[1024,512]{1,0:T(8,128)(2,1)} %all-gather.4.cloned.1.call-done), kind=kOutput, calls=%fused_computation.3 | convolution fusion | flops 4305453056 | bytes 38797312 | tf_op jit(solution)/shard_map/dot_general | solution.py:32
  118.7 0.0 reduce-scatter.2.cloned.1.call-update
  118.7 0.0 all-gather.8.cloned.1.call-start
  118.8 186.1 %reduce-scatter.2.cloned.1.call-done = f32[64,2,2048]{2,0,1:T(8,128)} async-done(((f32[1024,2,2048]{2,0,1:T(8,128)}), f32[64,2,2048]{2,0,1:T(8,128)}) %reduce-scatter.2.cloned.1.call-update) | async-done | bytes 1048592 | tf_op jit(solution)/shard_map/reduce_scatter | solution.py:31
  304.9 2.7 collective-permute-start
  307.6 24.0 %collective-permute-done = f32[64,2,2048]{2,0,1:T(8,128)S(1)} collective-permute-done((f32[64,2,2048]{2,0,1:T(8,128)}, f32[64,2,2048]{2,0,1:T(8,128)S(1)}, u32[]{:S(2)}, u32[]{:S(2)}) %collective-permute-start) | collective-permute-done | bytes 1048608 | tf_op jit(solution)/shard_map/ppermute | solution.py:8
  331.5 1.4 broadcast_select_fusion.1
  333.0 1.2 select_convert_fusion
  334.2 9.8 %constant_dynamic-slice_fusion = s32[512,1,2048]{2,1,0:T(1,128)} fusion(s32[512,2,2048]{2,1,0:T(2,128)} %param.6, s32[]{:T(128)S(6)} %select_n.43), kind=kLoop, calls=%fused_computation.22 | loop fusion | bytes 8388612 | tf_op jit(solution)/shard_map/jit(dynamic_index_in_dim)/dynamic_slice | solution.py:57
  344.0 64.9 %all-gather.8.cloned.1.call-done = bf16[1024,2048]{1,0:T(8,128)(2,1)} async-done(((bf16[64,2048]{1,0:T(8,128)(2,1)}), bf16[1024,2048]{1,0:T(8,128)(2,1)}) %all-gather.8.cloned.1.call-update) | async-done | bytes 4194320 | tf_op jit(solution)/shard_map/all_gather | solution.py:53
  408.9 7.1 %bitcast_reduce_fusion = f32[4,2048]{1,0:T(4,128)S(1)} fusion(s32[512,1,2048]{2,1,0:T(1,128)} %constant_dynamic-slice_fusion, bf16[1024,512]{1,0:T(8,128)(2,1)S(1)} %copy-done.2, bf16[1024,2048]{1,0:T(8,128)(2,1)} %all-gather.8.cloned.1.call-done), kind=kOutput, calls=%fused_computation.8 | convolution fusion | flops 2151669760 | bytes 9469952 | tf_op jit(solution)/shard_map/dot_general | solution.py:51
  416.0 0.6 broadcast_in_dim.7
  (8 shorter events, 0.0 us)
Async XLA Ops:
  6.5 1.6 copy-start
  6.5 68.9 %all-gather.6.cloned.1.call-start = ((), (), s32[]{:S(2)}) async-start(), calls=%async_computation.2 | async-start | bytes 6291456 | tf_op jit(solution)/shard_map/all_gather | solution.py:26
  7.3 93.8 %all-gather.4.cloned.1.call-start = ((), (), s32[]{:S(2)}) async-start(), calls=%async_computation.1 | async-start | bytes 1179648 | tf_op jit(solution)/shard_map/all_gather | solution.py:24
  8.8 296.1 %reduce-scatter.2.cloned.1.call-start = ((), (), s32[]{:S(2)}) async-start(), calls=%async_computation.3 | async-start | bytes 17825792 | tf_op jit(solution)/shard_map/reduce_scatter | solution.py:31
  118.7 290.2 %all-gather.8.cloned.1.call-start = ((), (), s32[]{:S(2)}) async-start(), calls=%async_computation.4 | async-start | bytes 4456448 | tf_op jit(solution)/shard_map/all_gather | solution.py:53
  304.9 26.7 %collective-permute-start = (f32[64,2,2048]{2,0,1:T(8,128)}, f32[64,2,2048]{2,0,1:T(8,128)S(1)}, u32[]{:S(2)}, u32[]{:S(2)}) collective-permute-start(f32[64,2,2048]{2,0,1:T(8,128)} %reduce-scatter.2.cloned.1.call-done), channel_id=1, source_target_pairs={{0,128},{128,0},{1,129},{129,1},{2,130},{130,2},{3,131},{131,3},{4... | collective-permute-start | bytes 3145736 | tf_op jit(solution)/shard_map/ppermute | solution.py:8
  334.2 74.8 %copy-start.2 = (bf16[1024,512]{1,0:T(8,128)(2,1)S(1)}, bf16[1024,512]{1,0:T(8,128)(2,1)}, u32[]{:S(2)}) copy-start(bf16[1024,512]{1,0:T(8,128)(2,1)} %all-gather.4.cloned.1.call-done) | copy-start | bytes 3145732
  334.2 82.5 %copy-start.1 = (bf16[128,8192]{1,0:T(8,128)(2,1)S(1)}, bf16[128,8192]{1,0:T(8,128)(2,1)}, u32[]{:S(2)}) copy-start(bf16[128,8192]{1,0:T(8,128)(2,1)} %param.4) | copy-start | bytes 6291460
Sparse Core Ops, SparseCore 0:
  9.2 66.1 all-gather.5
  77.3 23.7 all-gather.3
  118.8 185.9 reduce-scatter.1
  334.3 74.5 all-gather.7
where the time goes:
time: 424 us; the launch traced here: 423 us
  waiting for transfers between devices  330 us (78%)
  local copies, waits for them, and re-layouts  49.4 us (12%)
  matrix products  24.8 us (6%)
  between operations  13.2 us (3%)
    reduce_scatter x1, waiting for transfers between devices, per_device(): lax.psum_scatter(jnp.dot(rows, flat, preferred_element_type=jnp.float32)....  186 us
    all_gather x1, waiting for transfers between devices, per_device(): lax.all_gather(own_grads, 'mp', axis=0, tiled=True)  64.9 us
    all_gather x1, waiting for transfers between devices, per_device(): both = lax.all_gather(full_weights, 'grp', axis=1, tiled=True)  35.2 us
    ppermute x1, waiting for transfers between devices, swapped(): lax.ppermute(x, axis, [(i, i ^ 1 << apart) for i in range(lax.axis_size(a...  24 us
    all_gather x1, waiting for transfers between devices, per_device(): x_cols = lax.all_gather(x_slice, 'dp', axis=0, tiled=True)  19.4 us
    dot_general x1, matrix products, per_device(): jnp.dot(rows, flat, preferred_element_type=jnp.float32)  17.7 us
    unnamed x8, local copies, waits for them, and re-layouts  15.6 us
    reshape x1, local copies, waits for them, and re-layouts, dequantize(): jnp.repeat(scale_part, group, axis=0)  10.4 us
  transfers between devices with their start and end apart: 5, of which 5 were waited for; matrix products, arithmetic and copies ran while one was open for 11% of the time, Pallas kernels for 0%

commit v1 on v0

v1 whole, which is shorter than its diff:
```python
import jax
import jax.numpy as jnp
from jax import lax
from jax.experimental import pallas as pl
from jax.experimental.pallas import tpu as pltpu
from jax.sharding import PartitionSpec as P

BF = jnp.bfloat16
F32 = jnp.float32
CHUNKS = 4
PERIOD = 3


def multiple(value, of=128):
    return pl.multiple_of(value, of)


def sigmoid(v):
    return 1.0 / (1.0 + jnp.exp(-v))


def kernel(
    hidden, full, codes, scales, out,
    x_all, x_turned, w_teacher, offsets, w_student, code_own, code_next, code_prev,
    scale_all, scale_in, send_offsets, partial, stage, landed, grads, results, gathered,
    local_sem, x_send, x_recv, t_send, t_recv, s_send, s_recv, c_send, c_recv,
    r_send, r_recv, g_send, g_recv, o_send, o_recv,
):
    hi = lax.axis_index("grp")
    dp = lax.axis_index("dp")
    mp = lax.axis_index("mp")
    lo, z = mp // 8, lax.rem(mp, 8)
    y, core = dp // 2, lax.rem(dp, 2)
    x = hi * 2 + lo
    way = 1 - 2 * core

    def at(x=x, y=y, z=z, core=core):
        return (x // 2, y * 2 + core, lax.rem(x, 2) * 8 + z)

    x_next, x_prev, x_far = lax.rem(x + 1, 4), lax.rem(x + 3, 4), lax.rem(x + 2, 4)
    y_fwd, y_bwd, y_far = lax.rem(y + 4 + way, 4), lax.rem(y + 4 - way, 4), lax.rem(y + 2, 4)

    def zed(step):
        return lax.rem(z + 8 + way * step, 8)

    sibling = at(core=1 - core)
    to_y_fwd, to_y_bwd = at(y=y_fwd), at(y=y_bwd)
    to_x = [at(x=x_next), at(x=x_prev), at(x=x_far)]
    x_of = [x_next, x_prev, x_far]
    to_z_fwd, to_z_bwd = at(z=zed(1)), at(z=zed(-1))

    sent = []

    def send(src, dst, send_sem, recv_sem, device):
        copy = pltpu.make_async_remote_copy(
            src_ref=src, dst_ref=dst, send_sem=send_sem, recv_sem=recv_sem,
            device_id=device, device_id_type=pl.DeviceIdType.MESH,
        )
        copy.start()
        sent.append(copy)

    def arrived(ref, send_sem, recv_sem):
        pltpu.make_async_remote_copy(
            src_ref=ref, dst_ref=ref, send_sem=send_sem, recv_sem=recv_sem,
            device_id=sibling, device_id_type=pl.DeviceIdType.MESH,
        ).wait_recv()

    def local(src, dst, index):
        copy = pltpu.make_async_copy(src, dst, local_sem.at[index])
        copy.start()
        return copy

    def token_rows(block):
        return x_all.at[pl.ds(multiple(block * 128), 128), :]

    def own_columns(ref, chunk):
        return ref.at[chunk, lo, :, pl.ds(multiple(hi * 128), 128)]

    def teacher_columns(which, chunk):
        return full.at[:, pl.ds(multiple(which * 512 + chunk * 128), 128)]

    hidden_copies = [
        local(
            hidden.at[:, pl.ds(multiple(z * 512 + half * 4096), 512)],
            x_all.at[pl.ds(multiple(dp * 128), 128), pl.ds(half * 512, 512)],
            half,
        )
        for half in range(2)
    ]
    next_copy = local(codes.at[:, x_next], code_next, 2)
    prev_copy = local(codes.at[:, x_prev], code_prev, 3)
    scale_copy = local(scales, scale_in, 4)
    own_copy = local(codes.at[:, x], code_own, 5)
    teacher_copies = [
        local(teacher_columns(x, c), own_columns(w_teacher, c), 6 + c) for c in range(CHUNKS)
    ]

    barrier = pltpu.get_barrier_semaphore()
    for device in [sibling, to_y_fwd, to_y_bwd, to_z_fwd, to_z_bwd] + to_x:
        pl.semaphore_signal(barrier, inc=1, device_id=device, device_id_type=pl.DeviceIdType.MESH)
    pl.semaphore_wait(barrier, 8)

    def send_teacher(c):
        for j in (2, 0, 1):
            send(teacher_columns(x_of[j], c), own_columns(w_teacher, c),
                 t_send.at[c, j], t_recv.at[c, j], to_x[j])

    def code_offsets(ref, c, k):
        rows = ref.reshape(512 * 8, 128)[pl.ds(c * 2 + k, 512, stride=8), :]
        return (rows.astype(F32) - 1.5).astype(BF)

    def send_student(c):
        for j, ref in ((0, code_next), (1, code_prev)):
            low, high = code_offsets(ref, c, 0), code_offsets(ref, c, 1)
            send_offsets[c, j] = jnp.where(hi == 0, low, high)
            send(send_offsets.at[c, j], own_columns(offsets, c),
                 s_send.at[c, j], s_recv.at[c, j], to_x[j])

    def own_offsets(c):
        for k in range(2):
            offsets[c, lo, :, k * 128:(k + 1) * 128] = code_offsets(code_own, c, k)

    send_teacher(0)
    for copy in hidden_copies:
        copy.wait()
    mine = token_rows(dp)
    send(mine, mine, x_send.at[0], x_recv.at[0], to_y_fwd)
    send(mine, mine, x_send.at[1], x_recv.at[1], to_y_bwd)
    send(mine, mine, x_send.at[2], x_recv.at[2], sibling)
    next_copy.wait()
    prev_copy.wait()
    send_student(0)
    scale_copy.wait()
    scale_all[lo] = scale_in[:, x]
    send(scale_in.at[:, x_next], scale_all.at[lo], c_send, c_recv, to_x[0])
    send_teacher(1)
    send_student(1)
    own_copy.wait()
    for c in range(CHUNKS):
        own_offsets(c)

    behind, ahead, far = (token_rows(b * 2 + core) for b in (y_bwd, y_fwd, y_far))
    arrived(behind, x_send.at[0], x_recv.at[0])
    send(behind, behind, x_send.at[3], x_recv.at[3], to_y_fwd)
    send(behind, behind, x_send.at[4], x_recv.at[4], sibling)
    arrived(ahead, x_send.at[1], x_recv.at[1])
    send(ahead, ahead, x_send.at[5], x_recv.at[5], sibling)
    arrived(far, x_send.at[3], x_recv.at[3])
    send(far, far, x_send.at[6], x_recv.at[6], sibling)
    other = 1 - core
    for b, i in ((y, 2), (y_fwd, 4), (y_bwd, 5), (y_far, 6)):
        arrived(token_rows(b * 2 + other), x_send.at[i], x_recv.at[i])

    def project(c):
        teacher_copies[c].wait()
        for j, origin in ((0, x_prev), (1, x_next), (2, x_far)):
            block = w_teacher.at[
                c, lax.rem(origin, 2), :, pl.ds(multiple((origin // 2) * 128), 128)
            ]
            arrived(block, t_send.at[c, j], t_recv.at[c, j])
        for j, origin in ((0, x_prev), (1, x_next)):
            block = offsets.at[
                c, lax.rem(origin, 2), :, pl.ds(multiple((origin // 2) * 128), 128)
            ]
            arrived(block, s_send.at[c, j], s_recv.at[c, j])
        if c == 0:
            arrived(scale_all.at[1 - lo], c_send, c_recv)
        if c + 2 < CHUNKS:
            send_teacher(c + 2)
            send_student(c + 2)
        for half in range(2):
            for group in range(4):
                line = jnp.concatenate(
                    [scale_all[half, group, c * 2 + k:c * 2 + k + 1, :] for k in range(2)], axis=1
                )
                rows = pl.ds(half * 512 + group * 128, 128)
                values = offsets[c, half, group * 128:(group + 1) * 128, :].astype(F32)
                w_student[rows, :] = (values * line).astype(BF)
        teacher = w_teacher.at[c].reshape(1024, 256)

        @pl.loop(0, 4)
        def _(i):
            tokens = x_all[pl.ds(multiple(i * 256, 256), 256), :]
            student_part = jnp.dot(tokens, w_student[...], preferred_element_type=F32)
            teacher_part = jnp.dot(tokens, teacher[...], preferred_element_type=F32)
            gap = student_part - teacher_part
            for h in range(2):
                part = slice(h * 128, (h + 1) * 128)
                partial[c, i * 2 + h, :, 0:256] = student_part[part]
                partial[c, i * 2 + h, :, 256:512] = gap[part]

        pass_on(c, 0, zed(4), None, to_z_fwd)
        pass_on(c, 4, zed(-3), None, to_z_bwd)

    def pass_on(c, index, owner, before, device):
        total = partial[c, owner]
        if before is not None:
            total = total + landed[c, before].astype(F32)
        stage[c, index] = total.astype(BF)
        send(stage.at[c, index], landed.at[c, index],
             r_send.at[c, index], r_recv.at[c, index], device)

    def summed(c, index):
        arrived(landed.at[c, index], r_send.at[c, index], r_recv.at[c, index])

    def reduce_step(c, step):
        summed(c, step - 1)
        if step < 4:
            pass_on(c, step, zed(4 - step), step - 1, to_z_fwd)
            summed(c, 3 + step)
            if step < 3:
                pass_on(c, 4 + step, zed(step - 3), 3 + step, to_z_bwd)
            return
        total = partial[c, z] + landed[c, 3].astype(F32) + landed[c, 6].astype(F32)
        gate, upper = total[:, 0:128], total[:, 128:256]
        teacher_gate, teacher_upper = gate - total[:, 256:384], upper - total[:, 384:512]
        sig = sigmoid(gate)
        student_hidden = gate * sig * upper
        teacher_hidden = teacher_gate * sigmoid(teacher_gate) * teacher_upper
        difference = (student_hidden - teacher_hidden) * (1.0 / 1024.0)
        grads[c, z, :, 0:128] = (difference * upper * sig * (1.0 + gate * (1.0 - sig))).astype(BF)
        grads[c, z, :, 128:256] = (difference * gate * sig).astype(BF)
        own = grads.at[c, z]
        send(own, own, g_send.at[c, 0], g_recv.at[c, 0], to_z_fwd)
        send(own, own, g_send.at[c, 4], g_recv.at[c, 4], to_z_bwd)

    def gather_step(c, step):
        block = grads.at[c, zed(-step)]
        arrived(block, g_send.at[c, step - 1], g_recv.at[c, step - 1])
        if step < 4:
            send(block, block, g_send.at[c, step], g_recv.at[c, step], to_z_fwd)
            block = grads.at[c, zed(step)]
            arrived(block, g_send.at[c, 3 + step], g_recv.at[c, 3 + step])
            if step < 3:
                send(block, block, g_send.at[c, 4 + step], g_recv.at[c, 4 + step], to_z_bwd)

    def turn():
        for i in range(8):
            rows = slice(i * 128, (i + 1) * 128)
            x_turned[:, rows] = x_all[rows, :].T

    def back(c):
        all_grads = grads.at[c].reshape(1024, 256)
        for half in range(2):
            rows = x_turned[half * 512:(half + 1) * 512, :]
            weight_grads = jnp.dot(rows, all_grads[...], preferred_element_type=F32)
            weighted = weight_grads * offsets[c, half].astype(F32)
            sums = weighted.reshape(4, 128, 256).sum(axis=1)
            for k in range(2):
                results[k, half, :, c * 128:(c + 1) * 128] = sums[:, k * 128:(k + 1) * 128]

    events = []
    for c in range(CHUNKS):
        start = c * PERIOD
        events.append((start, c, project, ()))
        for step in range(1, 5):
            events.append((start + step, c, reduce_step, (step,)))
            events.append((start + 4 + step, c, gather_step, (step,)))
        events.append((start + 9, c, back, ()))
    turned = False
    for _, c, action, rest in sorted(events, key=lambda e: e[:2]):
        action(c, *rest)
        if not turned:
            turn()
            turned = True

    for j in range(3):
        send(results.at[x_of[j] // 2, lax.rem(x_of[j], 2)], gathered.at[x],
             o_send.at[j], o_recv.at[j], to_x[j])
    gathered[x] = results[hi, lo]
    for j, origin in ((0, x_prev), (1, x_next), (2, x_far)):
        arrived(gathered.at[origin], o_send.at[j], o_recv.at[j])
    for i in range(4):
        out[:, i * 512:(i + 1) * 512] = gathered[i]
    for copy in sent:
        copy.wait_send()


def tiles_of(array):
    rows = array.shape[0]
    return array.reshape(rows, 2, 4, 4, 128).transpose(0, 2, 3, 1, 4).reshape(rows, 4, 8, 128)


def per_device(hidden_in, full_weights, codes, scales):
    dma = pltpu.SemaphoreType.DMA
    out = pl.pallas_call(
        kernel,
        out_shape=jax.ShapeDtypeStruct((4, 2048), F32),
        in_specs=[pl.BlockSpec(memory_space=pl.ANY)] * 4,
        out_specs=pl.BlockSpec(memory_space=pltpu.VMEM),
        scratch_shapes=[
            pltpu.VMEM((1024, 1024), BF),
            pltpu.VMEM((1024, 1024), BF),
            pltpu.VMEM((CHUNKS, 2, 512, 256), BF),
            pltpu.VMEM((CHUNKS, 2, 512, 256), BF),
            pltpu.VMEM((1024, 256), BF),
            pltpu.VMEM((512, 8, 128), jnp.int32),
            pltpu.VMEM((512, 8, 128), jnp.int32),
            pltpu.VMEM((512, 8, 128), jnp.int32),
            pltpu.VMEM((2, 4, 8, 128), F32),
            pltpu.VMEM((4, 4, 8, 128), F32),
            pltpu.VMEM((CHUNKS, 2, 512, 128), BF),
            pltpu.VMEM((CHUNKS, 8, 128, 512), F32),
            pltpu.VMEM((CHUNKS, 7, 128, 512), BF),
            pltpu.VMEM((CHUNKS, 7, 128, 512), BF),
            pltpu.VMEM((CHUNKS, 8, 128, 256), BF),
            pltpu.VMEM((2, 2, 4, 512), F32),
            pltpu.VMEM((4, 4, 512), F32),
            dma((6 + CHUNKS,)),
            dma((7,)), dma((7,)),
            dma((CHUNKS, 3)), dma((CHUNKS, 3)),
            dma((CHUNKS, 2)), dma((CHUNKS, 2)),
            dma, dma,
            dma((CHUNKS, 7)), dma((CHUNKS, 7)),
            dma((CHUNKS, 7)), dma((CHUNKS, 7)),
            dma((3,)), dma((3,)),
        ],
        compiler_params=pltpu.CompilerParams(
            collective_id=0, has_side_effects=True, vmem_limit_bytes=60 * 1024 * 1024
        ),
        cost_estimate=pl.CostEstimate(
            flops=6 * 1024 ** 3, bytes_accessed=12 * 1024 ** 2, transcendentals=2 * 1024 * 512
        ),
    )(hidden_in, full_weights.reshape(512, 2048), tiles_of(codes), tiles_of(scales))
    return out[:, None, :]


def solution(mesh):
    return jax.shard_map(
        per_device,
        mesh=mesh,
        in_specs=(P("dp", None), P("mp", "grp", "dp"), P("mp", None, "dp"), P("mp", None, "dp")),
        out_specs=P("mp", "grp", "dp"),
        check_vma=False,
    )
```

time: 424 us -> 118 us (0.28)
  waiting for transfers between devices: 330 us -> 0 us
  Pallas kernels: 0 us -> 117 us
  local copies, waits for them, and re-layouts: 49.4 us -> 1.41 us
  matrix products: 24.8 us -> 0 us
  between operations: 13.2 us -> 0.01 us
    reduce_scatter x1 -> x0, waiting for transfers between devices: 186 us -> none  [per_device(): lax.psum_scatter(jnp.dot(rows, flat, preferred_element_type=jnp.float32)....]
    all_gather x3 -> x0, waiting for transfers between devices: 120 us -> none  [the longest x1 64.9 us: per_device(): lax.all_gather(own_grads, 'mp', axis=0, tiled=True)]
    pallas_call x0 -> x1, Pallas kernels: none -> 117 us  [per_device(): pl.pallas_call(kernel, out_shape=jax.ShapeDtypeStruct((4, 2048), F32), in...]
    dot_general x2 -> x0, matrix products: 24.8 us -> none  [the longest x1 17.7 us: per_device(): jnp.dot(rows, flat, preferred_element_type=jnp.float32)]
    ppermute x1 -> x0, waiting for transfers between devices: 24 us -> none  [swapped(): lax.ppermute(x, axis, [(i, i ^ 1 << apart) for i in range(lax.axis_size(a...]
    unnamed x8 -> x0, local copies, waits for them, and re-layouts: 15.6 us -> none
    dynamic_slice x2 -> x0, local copies, waits for them, and re-layouts: 10.5 us -> none  [the longest x1 9.82 us: per_device(): lax.dynamic_index_in_dim(codes, side, 1, keepdims=False).astype(jnp.float32)]
    reshape x1 -> x0, local copies, waits for them, and re-layouts: 10.4 us -> none  [dequantize(): jnp.repeat(scale_part, group, axis=0)]
  transfers between devices with their start and end apart: 5 -> 0, of which waited for: 5 -> 0; matrix products, arithmetic and copies ran while one was open for 11% -> 0% of each run, Pallas kernels for 0% -> 0%
where the time goes in v1:
time: 118 us
  Pallas kernels  117 us (99%)
  local copies, waits for them, and re-layouts  1.41 us (1%)
    pallas_call x1, Pallas kernels, per_device(): pl.pallas_call(kernel, out_shape=jax.ShapeDtypeStruct((4, 2048), F32), in...  117 us

profile of v1, /device:TPU:8, one launch (start us, length us, event | category | flops | bytes accessed | tf_op | source)
XLA Modules:
  0.0 118.2 jit_solution(5914091489830463643)
XLA Ops:
  0.0 116.8 %shard_map.46 = f32[4,2048]{1,0:T(4,128)} custom-call(bf16[128,8192]{1,0:T(8,128)(2,1)} %hidden.1, bf16[512,2048]{1,0:T(8,128)(2,1)} %bitcast.14, s32[512,4,8,128]{3,2,1,0:T(8,128)} %bitcast.13, f32[4,4,8,128]{3,2,1,0:T(8,128)} %bitcast.15), custom_call_target="tpu_custom_call" | custom-call | flops 6442450944 | bytes 12582912 | tf_op jit(solution)/shard_map/pallas_call | solution.py:286
  116.8 1.4 %copy.7 = f32[4,1,2048]{2,1,0:T(1,128)} copy(f32[4,1,2048]{2,0,1:T(4,128)} %bitcast.12) | data formatting | bytes 65536 | tf_op jit(solution)/shard_map/broadcast_in_dim | solution.py:325

commit v2 on v1

--- a/solution.py
+++ b/solution.py
@@ -8,7 +8,10 @@
 BF = jnp.bfloat16
 F32 = jnp.float32
 CHUNKS = 4
-PERIOD = 3
+PARTS = 1
+ROWS = 128 // PARTS
+PERIOD = 1.0
+SHIFT = 0.0
 
 
 def multiple(value, of=128):
@@ -44,7 +47,7 @@
         return lax.rem(z + 8 + way * step, 8)
 
     sibling = at(core=1 - core)
-    to_y_fwd, to_y_bwd = at(y=y_fwd), at(y=y_bwd)
+    to_y_fwd, to_y_bwd, to_y_far = at(y=y_fwd), at(y=y_bwd), at(y=y_far)
     to_x = [at(x=x_next), at(x=x_prev), at(x=x_far)]
     x_of = [x_next, x_prev, x_far]
     to_z_fwd, to_z_bwd = at(z=zed(1)), at(z=zed(-1))
@@ -96,9 +99,9 @@
     ]
 
     barrier = pltpu.get_barrier_semaphore()
-    for device in [sibling, to_y_fwd, to_y_bwd, to_z_fwd, to_z_bwd] + to_x:
+    for device in [sibling, to_y_fwd, to_y_bwd, to_y_far, to_z_fwd, to_z_bwd] + to_x:
         pl.semaphore_signal(barrier, inc=1, device_id=device, device_id_type=pl.DeviceIdType.MESH)
-    pl.semaphore_wait(barrier, 8)
+    pl.semaphore_wait(barrier, 9)
 
     def send_teacher(c):
         for j in (2, 0, 1):
@@ -126,6 +129,7 @@
     mine = token_rows(dp)
     send(mine, mine, x_send.at[0], x_recv.at[0], to_y_fwd)
     send(mine, mine, x_send.at[1], x_recv.at[1], to_y_bwd)
+    send(mine, mine, x_send.at[3], x_recv.at[3], to_y_far)
     send(mine, mine, x_send.at[2], x_recv.at[2], sibling)
     next_copy.wait()
     prev_copy.wait()
@@ -141,7 +145,6 @@
 
     behind, ahead, far = (token_rows(b * 2 + core) for b in (y_bwd, y_fwd, y_far))
     arrived(behind, x_send.at[0], x_recv.at[0])
-    send(behind, behind, x_send.at[3], x_recv.at[3], to_y_fwd)
     send(behind, behind, x_send.at[4], x_recv.at[4], sibling)
     arrived(ahead, x_send.at[1], x_recv.at[1])
     send(ahead, ahead, x_send.at[5], x_recv.at[5], sibling)
@@ -189,50 +192,60 @@
                 partial[c, i * 2 + h, :, 0:256] = student_part[part]
                 partial[c, i * 2 + h, :, 256:512] = gap[part]
 
-        pass_on(c, 0, zed(4), None, to_z_fwd)
-        pass_on(c, 4, zed(-3), None, to_z_bwd)
-
-    def pass_on(c, index, owner, before, device):
-        total = partial[c, owner]
+    def begin(c, part):
+        pass_on(c, part, 0, zed(4), None, to_z_fwd)
+        pass_on(c, part, 4, zed(-3), None, to_z_bwd)
+
+    def lines(part):
+        return slice(part * ROWS, (part + 1) * ROWS)
+
+    def pass_on(c, part, index, owner, before, device):
+        total = partial[c, owner, lines(part), :]
         if before is not None:
-            total = total + landed[c, before].astype(F32)
-        stage[c, index] = total.astype(BF)
-        send(stage.at[c, index], landed.at[c, index],
-             r_send.at[c, index], r_recv.at[c, index], device)
-
-    def summed(c, index):
-        arrived(landed.at[c, index], r_send.at[c, index], r_recv.at[c, index])
-
-    def reduce_step(c, step):
-        summed(c, step - 1)
+            total = total + landed[c, part, before].astype(F32)
+        stage[c, part, index] = total.astype(BF)
+        send(stage.at[c, part, index], landed.at[c, part, index],
+             r_send.at[c, part, index], r_recv.at[c, part, index], device)
+
+    def summed(c, part, index):
+        arrived(landed.at[c, part, index], r_send.at[c, part, index], r_recv.at[c, part, index])
+
+    def reduce_step(c, part, step):
+        summed(c, part, step - 1)
         if step < 4:
-            pass_on(c, step, zed(4 - step), step - 1, to_z_fwd)
-            summed(c, 3 + step)
+            pass_on(c, part, step, zed(4 - step), step - 1, to_z_fwd)
+            summed(c, part, 3 + step)
             if step < 3:
-                pass_on(c, 4 + step, zed(step - 3), 3 + step, to_z_bwd)
+                pass_on(c, part, 4 + step, zed(step - 3), 3 + step, to_z_bwd)
             return
-        total = partial[c, z] + landed[c, 3].astype(F32) + landed[c, 6].astype(F32)
+        total = (partial[c, z, lines(part), :] + landed[c, part, 3].astype(F32)
+                 + landed[c, part, 6].astype(F32))
         gate, upper = total[:, 0:128], total[:, 128:256]
         teacher_gate, teacher_upper = gate - total[:, 256:384], upper - total[:, 384:512]
         sig = sigmoid(gate)
         student_hidden = gate * sig * upper
         teacher_hidden = teacher_gate * sigmoid(teacher_gate) * teacher_upper
         difference = (student_hidden - teacher_hidden) * (1.0 / 1024.0)
-        grads[c, z, :, 0:128] = (difference * upper * sig * (1.0 + gate * (1.0 - sig))).astype(BF)
-        grads[c, z, :, 128:256] = (difference * gate * sig).astype(BF)
-        own = grads.at[c, z]
-        send(own, own, g_send.at[c, 0], g_recv.at[c, 0], to_z_fwd)
-        send(own, own, g_send.at[c, 4], g_recv.at[c, 4], to_z_bwd)
-
-    def gather_step(c, step):
-        block = grads.at[c, zed(-step)]
-        arrived(block, g_send.at[c, step - 1], g_recv.at[c, step - 1])
+        grads[c, z, lines(part), 0:128] = (difference * upper * sig * (1.0 + gate * (1.0 - sig))).astype(BF)
+        grads[c, z, lines(part), 128:256] = (difference * gate * sig).astype(BF)
+        share(c, part, z, 0, to_z_fwd)
+        share(c, part, z, 4, to_z_bwd)
+
+    def share(c, part, owner, index, device):
+        block = grads.at[c, owner, lines(part), :]
+        send(block, block, g_send.at[c, part, index], g_recv.at[c, part, index], device)
+
+    def shared(c, part, owner, index):
+        arrived(grads.at[c, owner, lines(part), :],
+                g_send.at[c, part, index], g_recv.at[c, part, index])
+
+    def gather_step(c, part, step):
+        shared(c, part, zed(-step), step - 1)
         if step < 4:
-            send(block, block, g_send.at[c, step], g_recv.at[c, step], to_z_fwd)
-            block = grads.at[c, zed(step)]
-            arrived(block, g_send.at[c, 3 + step], g_recv.at[c, 3 + step])
+            share(c, part, zed(-step), step, to_z_fwd)
+            shared(c, part, zed(step), 3 + step)
             if step < 3:
-                send(block, block, g_send.at[c, 4 + step], g_recv.at[c, 4 + step], to_z_bwd)
+                share(c, part, zed(step), 4 + step, to_z_bwd)
 
     def turn():
         for i in range(8):
@@ -253,16 +266,20 @@
     for c in range(CHUNKS):
         start = c * PERIOD
         events.append((start, c, project, ()))
-        for step in range(1, 5):
-            events.append((start + step, c, reduce_step, (step,)))
-            events.append((start + 4 + step, c, gather_step, (step,)))
-        events.append((start + 9, c, back, ()))
-    turned = False
+        for part in range(PARTS):
+            begun = start + part * SHIFT
+            events.append((begun, c, begin, (part,)))
+            for step in range(1, 5):
+                events.append((begun + step, c, reduce_step, (part, step)))
+                events.append((begun + 4 + step, c, gather_step, (part, step)))
+        events.append((start + (PARTS - 1) * SHIFT + 8.5, c, back, ()))
+    turned = 0
     for _, c, action, rest in sorted(events, key=lambda e: e[:2]):
         action(c, *rest)
-        if not turned:
+        turned += action is begin
+        if turned == PARTS:
             turn()
-            turned = True
+            turned += 1
 
     for j in range(3):
         send(results.at[x_of[j] // 2, lax.rem(x_of[j], 2)], gathered.at[x],
@@ -301,8 +318,8 @@
             pltpu.VMEM((4, 4, 8, 128), F32),
             pltpu.VMEM((CHUNKS, 2, 512, 128), BF),
             pltpu.VMEM((CHUNKS, 8, 128, 512), F32),
-            pltpu.VMEM((CHUNKS, 7, 128, 512), BF),
-            pltpu.VMEM((CHUNKS, 7, 128, 512), BF),
+            pltpu.VMEM((CHUNKS, PARTS, 7, ROWS, 512), BF),
+            pltpu.VMEM((CHUNKS, PARTS, 7, ROWS, 512), BF),
             pltpu.VMEM((CHUNKS, 8, 128, 256), BF),
             pltpu.VMEM((2, 2, 4, 512), F32),
             pltpu.VMEM((4, 4, 512), F32),
@@ -311,8 +328,8 @@
             dma((CHUNKS, 3)), dma((CHUNKS, 3)),
             dma((CHUNKS, 2)), dma((CHUNKS, 2)),
             dma, dma,
-            dma((CHUNKS, 7)), dma((CHUNKS, 7)),
-            dma((CHUNKS, 7)), dma((CHUNKS, 7)),
+            dma((CHUNKS, PARTS, 7)), dma((CHUNKS, PARTS, 7)),
+            dma((CHUNKS, PARTS, 7)), dma((CHUNKS, PARTS, 7)),
             dma((3,)), dma((3,)),
         ],
         compiler_params=pltpu.CompilerParams(

time: 118 us -> 101 us (0.86); the launches traced: 118 us -> 99.5 us
  Pallas kernels: 117 us -> 98.1 us
    pallas_call x1, Pallas kernels: 117 us -> 98.1 us  [per_device(): pl.pallas_call(kernel, out_shape=jax.ShapeDtypeStruct((4, 2048), F32), in...]
where the time goes in v2:
time: 101 us; the launch traced here: 99.5 us
  Pallas kernels  98.1 us (97%)
  local copies, waits for them, and re-layouts  1.41 us (1%)
    pallas_call x1, Pallas kernels, per_device(): pl.pallas_call(kernel, out_shape=jax.ShapeDtypeStruct((4, 2048), F32), in...  98.1 us

profile of v2, /device:TPU:8, one launch (start us, length us, event | category | flops | bytes accessed | tf_op | source)
XLA Modules:
  0.0 99.5 jit_solution(10335646550611702972)
XLA Ops:
  0.0 98.1 %shard_map.46 = f32[4,2048]{1,0:T(4,128)} custom-call(bf16[128,8192]{1,0:T(8,128)(2,1)} %hidden.1, bf16[512,2048]{1,0:T(8,128)(2,1)} %bitcast.14, s32[512,4,8,128]{3,2,1,0:T(8,128)} %bitcast.13, f32[4,4,8,128]{3,2,1,0:T(8,128)} %bitcast.15), custom_call_target="tpu_custom_call" | custom-call | flops 6442450944 | bytes 12582912 | tf_op jit(solution)/shard_map/pallas_call | solution.py:303
  98.1 1.4 %copy.7 = f32[4,1,2048]{2,1,0:T(1,128)} copy(f32[4,1,2048]{2,0,1:T(4,128)} %bitcast.12) | data formatting | bytes 65536 | tf_op jit(solution)/shard_map/broadcast_in_dim | solution.py:342

commit v3 on v1

v3 whole, which is shorter than its diff:
```python
import jax
import jax.numpy as jnp
from jax import lax
from jax.experimental import pallas as pl
from jax.experimental.pallas import tpu as pltpu
from jax.sharding import PartitionSpec as P

BF = jnp.bfloat16
F32 = jnp.float32
CHUNKS = 4
STARTS = (0, 1, 2, 3)
EARLY = 4
STRIDES = (3,)
LAG = 0.0
NEWEST = 1
HALVES = [(0, 2, 0, 512), (2, 4, 0, 512)]
WHOLE = [(0, 4, 0, 512)]
MESSAGES = (HALVES, WHOLE, WHOLE, WHOLE)
PLACE = (0, 1, 3, 2)


def multiple(value, of=128):
    return pl.multiple_of(value, of)


def sigmoid(v):
    return 1.0 / (1.0 + jnp.exp(-v))


def kernel(
    hidden, full, codes, scales, out,
    x_all, x_turned, w_teacher, offsets, w_student, code_own, code_next, code_prev,
    scale_all, scale_in, send_offsets, partial, stage, landed, grads, results, gathered,
    local_sem, y_send, y_recv, p_send, p_recv, t_send, t_recv, s_send, s_recv, c_send, c_recv,
    r_send, r_recv, g_send, g_recv, o_send, o_recv,
):
    hi = lax.axis_index("grp")
    dp = lax.axis_index("dp")
    mp = lax.axis_index("mp")
    lo, z = mp // 8, lax.rem(mp, 8)
    y, core = dp // 2, lax.rem(dp, 2)
    x = hi * 2 + lo
    way = 1 - 2 * core

    def at(x=x, y=y, z=z, core=core):
        return (x // 2, y * 2 + core, lax.rem(x, 2) * 8 + z)

    x_next, x_prev, x_far = lax.rem(x + 1, 4), lax.rem(x + 3, 4), lax.rem(x + 2, 4)

    def zed(step):
        return lax.rem(z + 8 + way * step, 8)

    def y_at(turn):
        return lax.rem(y + turn, 4)

    sibling = at(core=1 - core)
    to_x = [at(x=x_next), at(x=x_prev), at(x=x_far)]
    x_of = [x_next, x_prev, x_far]
    to_y = {turn: at(y=y_at(turn)) for turn in (1, 3)}
    to_relay = at(y=lax.rem(y + 4 - way, 4))
    to_z_fwd, to_z_bwd = at(z=zed(1)), at(z=zed(-1))
    to_z_fwd2, to_z_bwd2 = at(z=zed(2)), at(z=zed(-2))

    sent = []

    def send(src, dst, send_sem, recv_sem, device):
        copy = pltpu.make_async_remote_copy(
            src_ref=src, dst_ref=dst, send_sem=send_sem, recv_sem=recv_sem,
            device_id=device, device_id_type=pl.DeviceIdType.MESH,
        )
        copy.start()
        sent.append(copy)

    def arrived(ref, send_sem, recv_sem):
        pltpu.make_async_remote_copy(
            src_ref=ref, dst_ref=ref, send_sem=send_sem, recv_sem=recv_sem,
            device_id=sibling, device_id_type=pl.DeviceIdType.MESH,
        ).wait_recv()

    def local(src, dst, index):
        copy = pltpu.make_async_copy(src, dst, local_sem.at[index])
        copy.start()
        return copy

    def token_rows(place, which):
        return x_all.at[pl.ds(multiple(place * 256 + which * 128), 128), :]

    def own_columns(ref, chunk):
        return ref.at[chunk, lo, :, pl.ds(multiple(hi * 128), 128)]

    def teacher_columns(which, chunk):
        return full.at[:, pl.ds(multiple(which * 512 + chunk * 128), 128)]

    hidden_copies = [
        local(
            hidden.at[:, pl.ds(multiple(z * 512 + half * 4096), 512)],
            x_all.at[pl.ds(multiple(core * 128), 128), pl.ds(half * 512, 512)],
            half,
        )
        for half in range(2)
    ]
    next_copy = local(codes.at[:, x_next], code_next, 2)
    prev_copy = local(codes.at[:, x_prev], code_prev, 3)
    scale_copy = local(scales, scale_in, 4)
    own_copy = local(codes.at[:, x], code_own, 5)
    teacher_copies = [
        local(teacher_columns(x, c), own_columns(w_teacher, c), 6 + c) for c in range(CHUNKS)
    ]

    barrier = pltpu.get_barrier_semaphore()
    for device in [sibling, to_z_fwd, to_z_bwd, to_z_fwd2, to_z_bwd2] + to_x + list(to_y.values()):
        pl.semaphore_signal(barrier, inc=1, device_id=device, device_id_type=pl.DeviceIdType.MESH)

    def send_teacher(c):
        for j in (2, 0, 1):
            send(teacher_columns(x_of[j], c), own_columns(w_teacher, c),
                 t_send.at[c, j], t_recv.at[c, j], to_x[j])

    def code_offsets(ref, c, k):
        rows = ref.reshape(512 * 8, 128)[pl.ds(c * 2 + k, 512, stride=8), :]
        return (rows.astype(F32) - 1.5).astype(BF)

    def prepare_student(c):
        for j, ref in ((0, code_next), (1, code_prev)):
            send_offsets[c, j] = code_offsets(ref, c, hi)

    def send_student(c):
        for j in range(2):
            send(send_offsets.at[c, j], own_columns(offsets, c),
                 s_send.at[c, j], s_recv.at[c, j], to_x[j])

    def own_offsets(c):
        for k in range(2):
            offsets[c, lo, :, k * 128:(k + 1) * 128] = code_offsets(code_own, c, k)

    next_copy.wait()
    prev_copy.wait()
    prepare_student(0)
    scale_copy.wait()
    for copy in hidden_copies:
        copy.wait()
    pl.semaphore_wait(barrier, 10)
    send_student(0)
    send(scale_in.at[:, x_next], scale_all.at[lo], c_send, c_recv, to_x[0])
    mine = token_rows(0, core)
    for turn in (3, 1):
        send(mine, token_rows(PLACE[4 - turn], core),
             y_send.at[4 - turn], y_recv.at[4 - turn], to_y[turn])
    send(mine, mine, p_send.at[0], p_recv.at[0], sibling)
    send_teacher(0)
    for c in range(1, EARLY):
        prepare_student(c)
        send_student(c)
        send_teacher(c)
    scale_all[lo] = scale_in[:, x]
    own_copy.wait()
    own_offsets(0)

    def take_tokens(turn):
        rows = token_rows(PLACE[turn], core)
        arrived(rows, y_send.at[turn], y_recv.at[turn])
        send(rows, rows, p_send.at[turn], p_recv.at[turn], sibling)

    def relay_tokens():
        send(token_rows(1 + core, core), token_rows(PLACE[2], core),
             y_send.at[2], y_recv.at[2], to_relay)

    def take_sibling(turn):
        arrived(token_rows(PLACE[turn], 1 - core), p_send.at[turn], p_recv.at[turn])

    def take_teacher(c):
        teacher_copies[c].wait()
        for j, origin in ((0, x_prev), (1, x_next), (2, x_far)):
            block = w_teacher.at[
                c, lax.rem(origin, 2), :, pl.ds(multiple((origin // 2) * 128), 128)
            ]
            arrived(block, t_send.at[c, j], t_recv.at[c, j])

    def take_student(c):
        for j, origin in ((0, x_prev), (1, x_next)):
            block = offsets.at[
                c, lax.rem(origin, 2), :, pl.ds(multiple((origin // 2) * 128), 128)
            ]
            arrived(block, s_send.at[c, j], s_recv.at[c, j])
        for half in range(2):
            for group in range(4):
                line = jnp.concatenate(
                    [scale_all[half, group, c * 2 + k:c * 2 + k + 1, :] for k in range(2)], axis=1
                )
                rows = pl.ds(half * 512 + group * 128, 128)
                values = offsets[c, half, group * 128:(group + 1) * 128, :].astype(F32)
                w_student[rows, :] = (values * line).astype(BF)

    def student_rows(c, place):
        tokens = x_all[pl.ds(multiple(place * 256, 256), 256), :]
        sums = jnp.dot(tokens, w_student[...], preferred_element_type=F32)
        partial[c, place, :, :, 0:256] = sums.reshape(8, 32, 256)

    def teacher_rows(c, place):
        tokens = x_all[pl.ds(multiple(place * 256, 256), 256), :]
        weights = w_teacher.at[c].reshape(1024, 256)
        sums = jnp.dot(tokens, weights[...], preferred_element_type=F32).reshape(8, 32, 256)
        partial[c, place, :, :, 256:512] = partial[c, place, :, :, 0:256] - sums

    def begin(c, part):
        pass_on(c, part, 0, zed(4), None, to_z_fwd)
        pass_on(c, part, 4, zed(-3), None, to_z_bwd)

    def project_first(c):
        arrived(scale_all.at[1 - lo], c_send, c_recv)
        take_student(c)
        take_sibling(0)
        student_rows(c, 0)
        take_tokens(1)
        take_tokens(3)
        relay_tokens()
        take_sibling(1)
        student_rows(c, 1)
        take_teacher(c)
        teacher_rows(c, 0)
        teacher_rows(c, 1)
        begin(c, 0)
        take_sibling(3)
        student_rows(c, 2)
        teacher_rows(c, 2)
        take_tokens(2)
        take_sibling(2)
        student_rows(c, 3)
        teacher_rows(c, 3)
        begin(c, 1)
        own_offsets(1)
        send_later(c)

    def send_later(c):
        if EARLY <= c + 2 < CHUNKS:
            prepare_student(c + 2)
            send_student(c + 2)
            send_teacher(c + 2)

    def project(c):
        if c == 0:
            project_first(c)
            return
        take_student(c)
        take_teacher(c)
        send_later(c)

        @pl.loop(0, 4)
        def _(i):
            student_rows(c, i)
            teacher_rows(c, i)

        for part in range(len(MESSAGES[c])):
            begin(c, part)
        if c + 1 < CHUNKS:
            own_offsets(c + 1)

    def piece(ref, c, part, index):
        start, stop, low, high = MESSAGES[c][part]
        return ref.at[c, index, start:stop, :, low:high]

    def own_sums(c, part, owner):
        start, stop, low, high = MESSAGES[c][part]
        return partial[c, start:stop, owner, :, low:high]

    def pass_on(c, part, index, owner, before, device):
        total = own_sums(c, part, owner)
        if before is not None:
            total = total + piece(landed, c, part, before)[...].astype(F32)
        source = piece(stage, c, part, index)
        source[...] = total.astype(BF)
        send(source, piece(landed, c, part, index),
             r_send.at[c, part, index], r_recv.at[c, part, index], device)

    def summed(c, part, index):
        arrived(piece(landed, c, part, index),
                r_send.at[c, part, index], r_recv.at[c, part, index])

    def reduce_step(c, part, step):
        summed(c, part, step - 1)
        pass_on(c, part, step, zed(4 - step), step - 1, to_z_fwd)
        summed(c, part, 3 + step)
        if step < 3:
            pass_on(c, part, 4 + step, zed(step - 3), 3 + step, to_z_bwd)

    def finish(c):
        for part in range(len(MESSAGES[c])):
            summed(c, part, 3)
        total = partial[c, :, z] + landed[c, 3].astype(F32) + landed[c, 6].astype(F32)
        gate, upper = total[:, :, 0:128], total[:, :, 128:256]
        teacher_gate, teacher_upper = gate - total[:, :, 256:384], upper - total[:, :, 384:512]
        sig = sigmoid(gate)
        student_hidden = gate * sig * upper
        teacher_hidden = teacher_gate * sigmoid(teacher_gate) * teacher_upper
        difference = (student_hidden - teacher_hidden) * (1.0 / 1024.0)
        grads[c, :, z, :, 0:128] = (difference * upper * sig * (1.0 + gate * (1.0 - sig))).astype(BF)
        grads[c, :, z, :, 128:256] = (difference * gate * sig).astype(BF)
        share(c, z, 0, to_z_fwd)
        share(c, z, 4, to_z_bwd)
        if c in STRIDES:
            share(c, z, 1, to_z_fwd2)
            share(c, z, 5, to_z_bwd2)

    def share(c, owner, index, device):
        block = grads.at[c, :, owner]
        send(block, block, g_send.at[c, index], g_recv.at[c, index], device)

    def shared(c, owner, index):
        arrived(grads.at[c, :, owner], g_send.at[c, index], g_recv.at[c, index])

    def stride_step(c, step):
        if step == 1:
            shared(c, zed(-2), 1)
            share(c, zed(-2), 2, to_z_fwd)
            share(c, zed(-2), 3, to_z_fwd2)
            shared(c, zed(2), 5)
            share(c, zed(2), 6, to_z_bwd)
        else:
            for index, distance in ((0, -1), (4, 1), (2, -3), (6, 3), (3, -4)):
                shared(c, zed(distance), index)

    def gather_step(c, step):
        shared(c, zed(-step), step - 1)
        if step < 4:
            share(c, zed(-step), step, to_z_fwd)
            shared(c, zed(step), 3 + step)
            if step < 3:
                share(c, zed(step), 4 + step, to_z_bwd)

    def turn():
        for i in range(8):
            rows = slice(i * 128, (i + 1) * 128)
            x_turned[:, rows] = x_all[rows, :].T

    def back(c):
        all_grads = grads.at[c].reshape(1024, 256)
        for half in range(2):
            rows = x_turned[half * 512:(half + 1) * 512, :]
            weight_grads = jnp.dot(rows, all_grads[...], preferred_element_type=F32)
            weighted = weight_grads * offsets[c, half].astype(F32)
            sums = weighted.reshape(4, 128, 256).sum(axis=1)
            for k in range(2):
                results[k, half, :, c * 128:(c + 1) * 128] = sums[:, k * 128:(k + 1) * 128]

    events = []
    for c in range(CHUNKS):
        start = STARTS[c]
        events.append((start, c, project, ()))
        for step in range(1, 4):
            for part in range(len(MESSAGES[c])):
                events.append((start + step, c, reduce_step, (part, step)))
        events.append((start + 4, c, finish, ()))
        for step in range(1, 5):
            when = start + 4 + step + LAG * (CHUNKS - 1 - c)
            if c not in STRIDES:
                events.append((when, c, gather_step, (step,)))
            elif step < 3:
                events.append((when, c, stride_step, (step,)))
        events.append((when + 0.5, c, back, ()))
    for at_time, c, action, rest in sorted(events, key=lambda e: (e[0], NEWEST * e[1])):
        action(c, *rest)
        if at_time == 0:
            turn()
        while at_time >= 6 and len(sent) > 16:
            sent.pop(0).wait_send()

    for j in range(3):
        send(results.at[x_of[j] // 2, lax.rem(x_of[j], 2)], gathered.at[x],
             o_send.at[j], o_recv.at[j], to_x[j])
    gathered[x] = results[hi, lo]
    for j, origin in ((0, x_prev), (1, x_next), (2, x_far)):
        arrived(gathered.at[origin], o_send.at[j], o_recv.at[j])
    for i in range(4):
        out[:, i * 512:(i + 1) * 512] = gathered[i]
    for copy in sent:
        copy.wait_send()


def tiles_of(array):
    rows = array.shape[0]
    return array.reshape(rows, 2, 4, 4, 128).transpose(0, 2, 3, 1, 4).reshape(rows, 4, 8, 128)


def per_device(hidden_in, full_weights, codes, scales):
    dma = pltpu.SemaphoreType.DMA
    out = pl.pallas_call(
        kernel,
        out_shape=jax.ShapeDtypeStruct((4, 2048), F32),
        in_specs=[pl.BlockSpec(memory_space=pl.ANY)] * 4,
        out_specs=pl.BlockSpec(memory_space=pltpu.VMEM),
        scratch_shapes=[
            pltpu.VMEM((1024, 1024), BF),
            pltpu.VMEM((1024, 1024), BF),
            pltpu.VMEM((CHUNKS, 2, 512, 256), BF),
            pltpu.VMEM((CHUNKS, 2, 512, 256), BF),
            pltpu.VMEM((1024, 256), BF),
            pltpu.VMEM((512, 8, 128), jnp.int32),
            pltpu.VMEM((512, 8, 128), jnp.int32),
            pltpu.VMEM((512, 8, 128), jnp.int32),
            pltpu.VMEM((2, 4, 8, 128), F32),
            pltpu.VMEM((4, 4, 8, 128), F32),
            pltpu.VMEM((CHUNKS, 2, 512, 128), BF),
            pltpu.VMEM((CHUNKS, 4, 8, 32, 512), F32),
            pltpu.VMEM((CHUNKS, 7, 4, 32, 512), BF),
            pltpu.VMEM((CHUNKS, 7, 4, 32, 512), BF),
            pltpu.VMEM((CHUNKS, 4, 8, 32, 256), BF),
            pltpu.VMEM((2, 2, 4, 512), F32),
            pltpu.VMEM((4, 4, 512), F32),
            dma((6 + CHUNKS,)),
            dma((4,)), dma((4,)),
            dma((4,)), dma((4,)),
            dma((CHUNKS, 3)), dma((CHUNKS, 3)),
            dma((CHUNKS, 2)), dma((CHUNKS, 2)),
            dma, dma,
            dma((CHUNKS, 2, 7)), dma((CHUNKS, 2, 7)),
            dma((CHUNKS, 7)), dma((CHUNKS, 7)),
            dma((3,)), dma((3,)),
        ],
        compiler_params=pltpu.CompilerParams(
            collective_id=0, has_side_effects=True, vmem_limit_bytes=60 * 1024 * 1024
        ),
        cost_estimate=pl.CostEstimate(
            flops=6 * 1024 ** 3, bytes_accessed=12 * 1024 ** 2, transcendentals=2 * 1024 * 512
        ),
    )(hidden_in, full_weights.reshape(512, 2048), tiles_of(codes), tiles_of(scales))
    return out[:, None, :]


def solution(mesh):
    return jax.shard_map(
        per_device,
        mesh=mesh,
        in_specs=(P("dp", None), P("mp", "grp", "dp"), P("mp", None, "dp"), P("mp", None, "dp")),
        out_specs=P("mp", "grp", "dp"),
        check_vma=False,
    )
```

time: 118 us -> 98.2 us (0.83)
  Pallas kernels: 117 us -> 95.8 us
    pallas_call x1, Pallas kernels: 117 us -> 95.8 us  [per_device(): pl.pallas_call(kernel, out_shape=jax.ShapeDtypeStruct((4, 2048), F32), in...]
where the time goes in v3:
time: 98.2 us; the launch traced here: 97.2 us
  Pallas kernels  95.8 us (98%)
  local copies, waits for them, and re-layouts  1.41 us (1%)
    pallas_call x1, Pallas kernels, per_device(): pl.pallas_call(kernel, out_shape=jax.ShapeDtypeStruct((4, 2048), F32), in...  95.8 us

profile of v3, /device:TPU:8, one launch (start us, length us, event | category | flops | bytes accessed | tf_op | source)
XLA Modules:
  0.0 97.2 jit_solution(9184052481662483325)
XLA Ops:
  0.0 95.8 %shard_map.46 = f32[4,2048]{1,0:T(4,128)} custom-call(bf16[128,8192]{1,0:T(8,128)(2,1)} %hidden.1, bf16[512,2048]{1,0:T(8,128)(2,1)} %bitcast.14, s32[512,4,8,128]{3,2,1,0:T(8,128)} %bitcast.13, f32[4,4,8,128]{3,2,1,0:T(8,128)} %bitcast.15), custom_call_target="tpu_custom_call" | custom-call | flops 6442450944 | bytes 12582912 | tf_op jit(solution)/shard_map/pallas_call | solution.py:386
  95.8 1.4 %copy.7 = f32[4,1,2048]{2,1,0:T(1,128)} copy(f32[4,1,2048]{2,0,1:T(4,128)} %bitcast.12) | data formatting | bytes 65536 | tf_op jit(solution)/shard_map/broadcast_in_dim | solution.py:426

commit v4 on v3

--- a/solution.py
+++ b/solution.py
@@ -11,7 +11,7 @@
 STARTS = (0, 1, 2, 3)
 EARLY = 4
 STRIDES = (3,)
-LAG = 0.0
+LAG = -0.3
 NEWEST = 1
 HALVES = [(0, 2, 0, 512), (2, 4, 0, 512)]
 WHOLE = [(0, 4, 0, 512)]

time: 98.2 us -> 97.7 us (level)
  no operation moved by 1% of the time
where the time goes in v4:
time: 97.7 us; the launch traced here: 97.2 us
  Pallas kernels  95.7 us (98%)
  local copies, waits for them, and re-layouts  1.41 us (1%)
    pallas_call x1, Pallas kernels, per_device(): pl.pallas_call(kernel, out_shape=jax.ShapeDtypeStruct((4, 2048), F32), in...  95.7 us

profile of v4, /device:TPU:8, one launch (start us, length us, event | category | flops | bytes accessed | tf_op | source)
XLA Modules:
  0.0 97.2 jit_solution(495143632285930749)
XLA Ops:
  0.0 95.7 %shard_map.46 = f32[4,2048]{1,0:T(4,128)} custom-call(bf16[128,8192]{1,0:T(8,128)(2,1)} %hidden.1, bf16[512,2048]{1,0:T(8,128)(2,1)} %bitcast.14, s32[512,4,8,128]{3,2,1,0:T(8,128)} %bitcast.13, f32[4,4,8,128]{3,2,1,0:T(8,128)} %bitcast.15), custom_call_target="tpu_custom_call" | custom-call | flops 6442450944 | bytes 12582912 | tf_op jit(solution)/shard_map/pallas_call | solution.py:386
  95.8 1.4 %copy.7 = f32[4,1,2048]{2,1,0:T(1,128)} copy(f32[4,1,2048]{2,0,1:T(4,128)} %bitcast.12) | data formatting | bytes 65536 | tf_op jit(solution)/shard_map/broadcast_in_dim | solution.py:426
